TPU v7x, 256 devices: a whole 4x4x8 slice. The times are simulated.
256 devices in a mesh: blk: 32 (over z, y_hi, core), group: 8 (over x, y_lo).
Axes of the slice: x: 4, y: 4 (y_hi: 2, y_lo: 2; y = y_hi * 2 + y_lo), z: 8, core: 2. Of those that a mesh axis runs over, the one named last changes fastest.
Arguments:
- quantized: bfloat16 [1024, 64, 128], P(('blk', 'group')), may hold values from -4 to 4
- block_scales: bfloat16 [1024, 64, 4], P(('blk', 'group')), may hold values from 0.25 to 4
- token_counts: int32 [1024], P(('blk', 'group')), may hold values from 8 to 64
- cluster_ids: int32 [1024], P(('blk', 'group')), may hold values from 0 to 255, as said below
Outputs:
- global_best: float32 [1024], P(('blk', 'group'))
- cluster_best: float32 [1024], P(('blk', 'group'))
Inputs may be any that keep to these rules, and one draw needn't show every extreme that they name: `cluster_ids`: every cluster holds two or more documents; every id from 0 to the maximum is used.
All inputs are finite; a program needn't handle non-finite values.
Results may differ from a plain program's by a relative error of at most 0.00039.
Values may be sent and summed in bfloat16 or wider, within the bound.
A program may use at most 128 MiB of HBM per device.

v0:
```python
import math

import jax
import jax.numpy as jnp
from jax import lax
from jax.sharding import PartitionSpec as P

NEG_FILL = -1e30


def from_behind(value, axis, steps):
    count = lax.axis_size(axis)
    pairs = [(source, (source + steps) % count) for source in range(count)]
    return lax.ppermute(value, axis, pairs)


def as_sent(array):

    def short(part):
        return part.astype(jnp.bfloat16) if part.dtype == jnp.float32 else part

    return jax.tree.map(short, array)


def dequantize(quantized, block_scales):
    doc_count, tok_count, feature_width = quantized.shape
    blocks = block_scales.shape[2]
    grouped = quantized.reshape(doc_count, tok_count, blocks, feature_width // blocks).astype(
        jnp.float32
    )
    scaled = grouped * block_scales.astype(jnp.float32)[:, :, :, None]
    return scaled.reshape(doc_count, tok_count, feature_width).astype(jnp.bfloat16)


def chamfer_direct(queries, query_mask, query_count, quantized, block_scales, key_counts, factor):
    key_values = dequantize(quantized, block_scales)
    key_docs, tok_count, feature_width = key_values.shape
    query_docs = query_mask.shape[0]
    products = lax.dot_general(
        queries,
        key_values.reshape(key_docs * tok_count, feature_width),
        (((1,), (1,)), ((), ())),
        preferred_element_type=jnp.float32,
    )
    scores = products.reshape(query_docs, tok_count, key_docs, tok_count) * factor
    key_mask = lax.broadcasted_iota(jnp.int32, (key_docs, tok_count), 1) < key_counts[:, None]
    row_max = jnp.max(jnp.where(key_mask[None, None, :, :], scores, NEG_FILL), axis=3)
    forward = (
        jnp.sum(jnp.where(query_mask[:, :, None], row_max, 0.0), axis=1) / query_count[:, None]
    )
    column_max = jnp.max(jnp.where(query_mask[:, :, None, None], scores, NEG_FILL), axis=1)
    backward = (
        jnp.sum(jnp.where(key_mask[None, :, :], column_max, 0.0), axis=2)
        / key_counts.astype(jnp.float32)[None, :]
    )
    return 0.5 * (forward + backward)


def section_size(key_docs, query_docs):
    section = max(1, min(key_docs, 256 // query_docs))
    while key_docs % section != 0:
        section = section - 1
    return section


def chamfer_piece(queries, query_mask, query_count, quantized, block_scales, key_counts, factor):
    key_docs = quantized.shape[0]
    query_docs = query_mask.shape[0]
    section = section_size(key_docs, query_docs)
    sections = key_docs // section
    stacked = (
        quantized.reshape((sections, section) + quantized.shape[1:]),
        block_scales.reshape((sections, section) + block_scales.shape[1:]),
        key_counts.reshape(sections, section),
    )

    def sub_block(section_piece):
        return chamfer_direct(
            queries,
            query_mask,
            query_count,
            section_piece[0],
            section_piece[1],
            section_piece[2],
            factor,
        )

    similar = lax.map(sub_block, stacked)
    return jnp.transpose(similar, (1, 0, 2)).reshape(query_docs, key_docs)


def absorb(carried, shard_piece, doc_ids, query_side, factor):
    queries, query_mask, query_count, query_ids, query_clusters = query_side
    similar = chamfer_piece(
        queries, query_mask, query_count, shard_piece[0], shard_piece[1], shard_piece[2], factor
    )
    distinct = doc_ids[None, :] != query_ids[:, None]
    partner = distinct & (shard_piece[3][None, :] == query_clusters[:, None])
    overall = jnp.maximum(carried[0], jnp.max(jnp.where(distinct, similar, NEG_FILL), axis=1))
    within = jnp.maximum(carried[1], jnp.max(jnp.where(partner, similar, NEG_FILL), axis=1))
    return (overall, within)


def query_setup(quantized, block_scales, token_counts, cluster_ids, query_ids):
    doc_count, tok_count, feature_width = quantized.shape
    queries = dequantize(quantized, block_scales).reshape(doc_count * tok_count, feature_width)
    query_mask = lax.broadcasted_iota(jnp.int32, (doc_count, tok_count), 1) < token_counts[:, None]
    return (queries, query_mask, token_counts.astype(jnp.float32), query_ids, cluster_ids)


def shards(quantized, block_scales, token_counts, cluster_ids):
    doc_count, tok_count, feature_width = quantized.shape
    factor = 1.0 / math.sqrt(feature_width)
    group_total = lax.axis_size("group")
    device_index = lax.axis_index("blk") * group_total + lax.axis_index("group")
    own_ids = device_index * doc_count + jnp.arange(doc_count, dtype=jnp.int32)
    own_side = query_setup(quantized, block_scales, token_counts, cluster_ids, own_ids)
    starting = (
        jnp.full((doc_count,), NEG_FILL, jnp.float32),
        jnp.full((doc_count,), NEG_FILL, jnp.float32),
    )

    def visit_group(turn_index, state):
        visiting, carried = state
        visiting = from_behind((visiting[0], visiting[1], visiting[2], visiting[3]), "group", 1)
        source_group = (lax.axis_index("group") - turn_index) % group_total
        shard_piece = (
            lax.all_gather(visiting[0], "blk", axis=0, tiled=True),
            lax.all_gather(visiting[1], "blk", axis=0, tiled=True),
            lax.all_gather(as_sent(visiting[2]), "blk", axis=0, tiled=True),
            lax.all_gather(as_sent(visiting[3]), "blk", axis=0, tiled=True),
        )
        piece_docs = shard_piece[0].shape[0]
        position = jnp.arange(piece_docs, dtype=jnp.int32)
        doc_ids = (
            position // doc_count * group_total + source_group
        ) * doc_count + position % doc_count
        carried = absorb(carried, shard_piece, doc_ids, own_side, factor)
        return (visiting, carried)

    finished, results = lax.fori_loop(
        1,
        group_total + 1,
        visit_group,
        ((quantized, block_scales, token_counts, cluster_ids), starting),
    )
    return (results[0], results[1])


def solution(mesh):
    placed = (
        P(("blk", "group"), None, None),
        P(("blk", "group"), None, None),
        P(("blk", "group")),
        P(("blk", "group")),
    )
    return jax.shard_map(
        shards,
        mesh=mesh,
        in_specs=placed,
        out_specs=(P(("blk", "group")), P(("blk", "group"))),
        check_vma=False,
    )
```

profile of v0, /device:TPU:1, one launch (start us, length us, event | category | flops | bytes accessed | tf_op | source)
XLA Modules:
  0.0 1241.2 jit_solution(640579858623119233)
XLA Ops:
  10.8 1223.0 %while.63 = (s32[]{:T(128)}, bf16[4,64,128]{2,1,0:T(8,128)(2,1)S(1)}, bf16[4,64,4]{1,2,0:T(4,128)(2,1)S(1)}, s32[4]{0:T(128)S(1)}, s32[4]{0:T(128)S(1)}, /*index...) while((s32[]{:T(128)}, ...), condition=%wide.region_9.10_spmd.clone, body=%wide.region_0.9_spmd.clone.sunk | while | flops 275312320 | bytes 40553048 | solution.py:141
  22.5 20.2 %all-reduce.6 = (s32[128]{0:T(128)S(1)}, s32[128]{0:T(128)S(1)}) all-reduce(s32[128]{0:T(128)S(1)} %dynamic-update-slice.6, s32[128]{0:T(128)S(1)} %dynamic-update-slice.7), channel_id=1, replica_groups=mesh['blk'=32,'group'=8] {'blk'}, use_global_device_ids=true, to_apply=%add | all-reduce | flops 256 | bytes 2048 | tf_op jit(solution)/shard_map/while
  42.8 43.1 %all_gather.49 = bf16[128,64,4]{1,2,0:T(4,128)(2,1)S(1)} all-gather(bf16[4,64,4]{1,2,0:T(4,128)(2,1)S(1)} %collective-permute-done.1), channel_id=1, replica_groups=mesh['blk'=32,'group'=8] {'blk'}, dimensions={0}, use_global_device_ids=true | all-gather | bytes 67584 | tf_op jit(solution)/shard_map/while/body/eval_jaxpr/all_gather | solution.py:129
  86.8 14.4 %all-gather.2.cloned.1.call-done = bf16[128,64,128]{2,1,0:T(8,128)(2,1)} async-done(((bf16[4,64,128]{2,1,0:T(8,128)(2,1)}), bf16[128,64,128]{2,1,0:T(8,128)(2,1)}) %all-gather.2.cloned.1.call-update) | async-done | bytes 2097168 | tf_op jit(solution)/shard_map/while/body/eval_jaxpr/all_gather | solution.py:128
  101.2 69.4 %while.64 = (s32[]{:T(128)}, f32[2,4,64]{1,2,0:T(8,128)S(1)}, pred[4,64]{1,0:T(4,128)(4,1)S(1)}, s32[2,64]{1,0:T(2,128)S(1)}, bf16[2,64,64,128]{3,2,1,0:T(8,128)...) while((s32[]{:T(128)}, f32[2,4,64]{1,2,0:T(8,128)S(1)}, ...), condition=%wide.region_6.6_spmd, body=%wide.region_1.5_spmd.sunk | while | flops 275305024 | bytes 33319532 | solution.py:88
  195.5 43.9 %all_gather.49 = bf16[128,64,4]{1,2,0:T(4,128)(2,1)S(1)} all-gather(bf16[4,64,4]{1,2,0:T(4,128)(2,1)S(1)} %collective-permute-done.1), channel_id=1, replica_groups=mesh['blk'=32,'group'=8] {'blk'}, dimensions={0}, use_global_device_ids=true | all-gather | bytes 67584 | tf_op jit(solution)/shard_map/while/body/eval_jaxpr/all_gather | solution.py:129
  252.9 69.4 %while.64 = (s32[]{:T(128)}, f32[2,4,64]{1,2,0:T(8,128)S(1)}, pred[4,64]{1,0:T(4,128)(4,1)S(1)}, s32[2,64]{1,0:T(2,128)S(1)}, bf16[2,64,64,128]{3,2,1,0:T(8,128)...) while((s32[]{:T(128)}, f32[2,4,64]{1,2,0:T(8,128)S(1)}, ...), condition=%wide.region_6.6_spmd, body=%wide.region_1.5_spmd.sunk | while | flops 275305024 | bytes 33319532 | solution.py:88
  347.8 43.4 %all_gather.49 = bf16[128,64,4]{1,2,0:T(4,128)(2,1)S(1)} all-gather(bf16[4,64,4]{1,2,0:T(4,128)(2,1)S(1)} %collective-permute-done.1), channel_id=1, replica_groups=mesh['blk'=32,'group'=8] {'blk'}, dimensions={0}, use_global_device_ids=true | all-gather | bytes 67584 | tf_op jit(solution)/shard_map/while/body/eval_jaxpr/all_gather | solution.py:129
  404.8 69.4 %while.64 = (s32[]{:T(128)}, f32[2,4,64]{1,2,0:T(8,128)S(1)}, pred[4,64]{1,0:T(4,128)(4,1)S(1)}, s32[2,64]{1,0:T(2,128)S(1)}, bf16[2,64,64,128]{3,2,1,0:T(8,128)...) while((s32[]{:T(128)}, f32[2,4,64]{1,2,0:T(8,128)S(1)}, ...), condition=%wide.region_6.6_spmd, body=%wide.region_1.5_spmd.sunk | while | flops 275305024 | bytes 33319532 | solution.py:88
  485.4 14.1 %all-reduce.6 = (s32[128]{0:T(128)S(1)}, s32[128]{0:T(128)S(1)}) all-reduce(s32[128]{0:T(128)S(1)} %dynamic-update-slice.6, s32[128]{0:T(128)S(1)} %dynamic-update-slice.7), channel_id=1, replica_groups=mesh['blk'=32,'group'=8] {'blk'}, use_global_device_ids=true, to_apply=%add | all-reduce | flops 256 | bytes 2048 | tf_op jit(solution)/shard_map/while
  499.7 43.4 %all_gather.49 = bf16[128,64,4]{1,2,0:T(4,128)(2,1)S(1)} all-gather(bf16[4,64,4]{1,2,0:T(4,128)(2,1)S(1)} %collective-permute-done.1), channel_id=1, replica_groups=mesh['blk'=32,'group'=8] {'blk'}, dimensions={0}, use_global_device_ids=true | all-gather | bytes 67584 | tf_op jit(solution)/shard_map/while/body/eval_jaxpr/all_gather | solution.py:129
  556.7 69.4 %while.64 = (s32[]{:T(128)}, f32[2,4,64]{1,2,0:T(8,128)S(1)}, pred[4,64]{1,0:T(4,128)(4,1)S(1)}, s32[2,64]{1,0:T(2,128)S(1)}, bf16[2,64,64,128]{3,2,1,0:T(8,128)...) while((s32[]{:T(128)}, f32[2,4,64]{1,2,0:T(8,128)S(1)}, ...), condition=%wide.region_6.6_spmd, body=%wide.region_1.5_spmd.sunk | while | flops 275305024 | bytes 33319532 | solution.py:88
  637.2 14.2 %all-reduce.6 = (s32[128]{0:T(128)S(1)}, s32[128]{0:T(128)S(1)}) all-reduce(s32[128]{0:T(128)S(1)} %dynamic-update-slice.6, s32[128]{0:T(128)S(1)} %dynamic-update-slice.7), channel_id=1, replica_groups=mesh['blk'=32,'group'=8] {'blk'}, use_global_device_ids=true, to_apply=%add | all-reduce | flops 256 | bytes 2048 | tf_op jit(solution)/shard_map/while
  651.6 43.3 %all_gather.49 = bf16[128,64,4]{1,2,0:T(4,128)(2,1)S(1)} all-gather(bf16[4,64,4]{1,2,0:T(4,128)(2,1)S(1)} %collective-permute-done.1), channel_id=1, replica_groups=mesh['blk'=32,'group'=8] {'blk'}, dimensions={0}, use_global_device_ids=true | all-gather | bytes 67584 | tf_op jit(solution)/shard_map/while/body/eval_jaxpr/all_gather | solution.py:129
  708.6 69.4 %while.64 = (s32[]{:T(128)}, f32[2,4,64]{1,2,0:T(8,128)S(1)}, pred[4,64]{1,0:T(4,128)(4,1)S(1)}, s32[2,64]{1,0:T(2,128)S(1)}, bf16[2,64,64,128]{3,2,1,0:T(8,128)...) while((s32[]{:T(128)}, f32[2,4,64]{1,2,0:T(8,128)S(1)}, ...), condition=%wide.region_6.6_spmd, body=%wide.region_1.5_spmd.sunk | while | flops 275305024 | bytes 33319532 | solution.py:88
  789.2 14.1 %all-reduce.6 = (s32[128]{0:T(128)S(1)}, s32[128]{0:T(128)S(1)}) all-reduce(s32[128]{0:T(128)S(1)} %dynamic-update-slice.6, s32[128]{0:T(128)S(1)} %dynamic-update-slice.7), channel_id=1, replica_groups=mesh['blk'=32,'group'=8] {'blk'}, use_global_device_ids=true, to_apply=%add | all-reduce | flops 256 | bytes 2048 | tf_op jit(solution)/shard_map/while
  803.5 43.4 %all_gather.49 = bf16[128,64,4]{1,2,0:T(4,128)(2,1)S(1)} all-gather(bf16[4,64,4]{1,2,0:T(4,128)(2,1)S(1)} %collective-permute-done.1), channel_id=1, replica_groups=mesh['blk'=32,'group'=8] {'blk'}, dimensions={0}, use_global_device_ids=true | all-gather | bytes 67584 | tf_op jit(solution)/shard_map/while/body/eval_jaxpr/all_gather | solution.py:129
  860.5 69.4 %while.64 = (s32[]{:T(128)}, f32[2,4,64]{1,2,0:T(8,128)S(1)}, pred[4,64]{1,0:T(4,128)(4,1)S(1)}, s32[2,64]{1,0:T(2,128)S(1)}, bf16[2,64,64,128]{3,2,1,0:T(8,128)...) while((s32[]{:T(128)}, f32[2,4,64]{1,2,0:T(8,128)S(1)}, ...), condition=%wide.region_6.6_spmd, body=%wide.region_1.5_spmd.sunk | while | flops 275305024 | bytes 33319532 | solution.py:88
  941.0 14.1 %all-reduce.6 = (s32[128]{0:T(128)S(1)}, s32[128]{0:T(128)S(1)}) all-reduce(s32[128]{0:T(128)S(1)} %dynamic-update-slice.6, s32[128]{0:T(128)S(1)} %dynamic-update-slice.7), channel_id=1, replica_groups=mesh['blk'=32,'group'=8] {'blk'}, use_global_device_ids=true, to_apply=%add | all-reduce | flops 256 | bytes 2048 | tf_op jit(solution)/shard_map/while
  955.4 43.4 %all_gather.49 = bf16[128,64,4]{1,2,0:T(4,128)(2,1)S(1)} all-gather(bf16[4,64,4]{1,2,0:T(4,128)(2,1)S(1)} %collective-permute-done.1), channel_id=1, replica_groups=mesh['blk'=32,'group'=8] {'blk'}, dimensions={0}, use_global_device_ids=true | all-gather | bytes 67584 | tf_op jit(solution)/shard_map/while/body/eval_jaxpr/all_gather | solution.py:129
  1012.4 69.4 %while.64 = (s32[]{:T(128)}, f32[2,4,64]{1,2,0:T(8,128)S(1)}, pred[4,64]{1,0:T(4,128)(4,1)S(1)}, s32[2,64]{1,0:T(2,128)S(1)}, bf16[2,64,64,128]{3,2,1,0:T(8,128)...) while((s32[]{:T(128)}, f32[2,4,64]{1,2,0:T(8,128)S(1)}, ...), condition=%wide.region_6.6_spmd, body=%wide.region_1.5_spmd.sunk | while | flops 275305024 | bytes 33319532 | solution.py:88
  1092.9 14.2 %all-reduce.6 = (s32[128]{0:T(128)S(1)}, s32[128]{0:T(128)S(1)}) all-reduce(s32[128]{0:T(128)S(1)} %dynamic-update-slice.6, s32[128]{0:T(128)S(1)} %dynamic-update-slice.7), channel_id=1, replica_groups=mesh['blk'=32,'group'=8] {'blk'}, use_global_device_ids=true, to_apply=%add | all-reduce | flops 256 | bytes 2048 | tf_op jit(solution)/shard_map/while
  1107.3 43.3 %all_gather.49 = bf16[128,64,4]{1,2,0:T(4,128)(2,1)S(1)} all-gather(bf16[4,64,4]{1,2,0:T(4,128)(2,1)S(1)} %collective-permute-done.1), channel_id=1, replica_groups=mesh['blk'=32,'group'=8] {'blk'}, dimensions={0}, use_global_device_ids=true | all-gather | bytes 67584 | tf_op jit(solution)/shard_map/while/body/eval_jaxpr/all_gather | solution.py:129
  1164.3 69.4 %while.64 = (s32[]{:T(128)}, f32[2,4,64]{1,2,0:T(8,128)S(1)}, pred[4,64]{1,0:T(4,128)(4,1)S(1)}, s32[2,64]{1,0:T(2,128)S(1)}, bf16[2,64,64,128]{3,2,1,0:T(8,128)...) while((s32[]{:T(128)}, f32[2,4,64]{1,2,0:T(8,128)S(1)}, ...), condition=%wide.region_6.6_spmd, body=%wide.region_1.5_spmd.sunk | while | flops 275305024 | bytes 33319532 | solution.py:88
  (543 shorter events, 768.1 us)
Async XLA Ops:
  10.8 90.4 %all-gather.2.cloned.1.call-start = ((), (), s32[]{:S(2)}) async-start(), calls=%async_computation | async-start | bytes 2162688 | tf_op jit(solution)/shard_map/while/body/eval_jaxpr/all_gather | solution.py:128
  10.8 6.0 collective-permute-start
  18.8 24.0 %collective-permute-start.1 = (bf16[4,64,4]{1,2,0:T(4,128)(2,1)S(1)}, bf16[4,64,4]{1,2,0:T(4,128)(2,1)S(1)}, u32[]{:S(2)}, u32[]{:S(2)}) collective-permute-start(bf16[4,64,4]{1,2,0:T(4,128)(2,1)S(1)} %get-tuple-element.742), channel_id=1, source_target_pairs={{0,1},{1,2},{2,3},{3,4},{4,5},{5,6},{6,7},{7,0},{8,9},{9,10},{10,1... | collective-permute-start | bytes 6152 | tf_op jit(solution)/shard_map/while/body/eval_jaxpr/ppermute | solution.py:14
  170.7 82.2 %all-gather.2.cloned.1.call-start = ((), (), s32[]{:S(2)}) async-start(), calls=%async_computation | async-start | bytes 2162688 | tf_op jit(solution)/shard_map/while/body/eval_jaxpr/all_gather | solution.py:128
  170.8 5.3 collective-permute-start
  178.0 17.5 %collective-permute-start.1 = (bf16[4,64,4]{1,2,0:T(4,128)(2,1)S(1)}, bf16[4,64,4]{1,2,0:T(4,128)(2,1)S(1)}, u32[]{:S(2)}, u32[]{:S(2)}) collective-permute-start(bf16[4,64,4]{1,2,0:T(4,128)(2,1)S(1)} %get-tuple-element.742), channel_id=1, source_target_pairs={{0,1},{1,2},{2,3},{3,4},{4,5},{5,6},{6,7},{7,0},{8,9},{9,10},{10,1... | collective-permute-start | bytes 6152 | tf_op jit(solution)/shard_map/while/body/eval_jaxpr/ppermute | solution.py:14
  322.5 82.3 %all-gather.2.cloned.1.call-start = ((), (), s32[]{:S(2)}) async-start(), calls=%async_computation | async-start | bytes 2162688 | tf_op jit(solution)/shard_map/while/body/eval_jaxpr/all_gather | solution.py:128
  322.5 5.3 collective-permute-start
  329.8 18.0 %collective-permute-start.1 = (bf16[4,64,4]{1,2,0:T(4,128)(2,1)S(1)}, bf16[4,64,4]{1,2,0:T(4,128)(2,1)S(1)}, u32[]{:S(2)}, u32[]{:S(2)}) collective-permute-start(bf16[4,64,4]{1,2,0:T(4,128)(2,1)S(1)} %get-tuple-element.742), channel_id=1, source_target_pairs={{0,1},{1,2},{2,3},{3,4},{4,5},{5,6},{6,7},{7,0},{8,9},{9,10},{10,1... | collective-permute-start | bytes 6152 | tf_op jit(solution)/shard_map/while/body/eval_jaxpr/ppermute | solution.py:14
  474.4 82.3 %all-gather.2.cloned.1.call-start = ((), (), s32[]{:S(2)}) async-start(), calls=%async_computation | async-start | bytes 2162688 | tf_op jit(solution)/shard_map/while/body/eval_jaxpr/all_gather | solution.py:128
  474.4 5.3 collective-permute-start
  481.6 18.1 %collective-permute-start.1 = (bf16[4,64,4]{1,2,0:T(4,128)(2,1)S(1)}, bf16[4,64,4]{1,2,0:T(4,128)(2,1)S(1)}, u32[]{:S(2)}, u32[]{:S(2)}) collective-permute-start(bf16[4,64,4]{1,2,0:T(4,128)(2,1)S(1)} %get-tuple-element.742), channel_id=1, source_target_pairs={{0,1},{1,2},{2,3},{3,4},{4,5},{5,6},{6,7},{7,0},{8,9},{9,10},{10,1... | collective-permute-start | bytes 6152 | tf_op jit(solution)/shard_map/while/body/eval_jaxpr/ppermute | solution.py:14
  626.2 82.4 %all-gather.2.cloned.1.call-start = ((), (), s32[]{:S(2)}) async-start(), calls=%async_computation | async-start | bytes 2162688 | tf_op jit(solution)/shard_map/while/body/eval_jaxpr/all_gather | solution.py:128
  626.3 5.3 collective-permute-start
  633.5 18.1 %collective-permute-start.1 = (bf16[4,64,4]{1,2,0:T(4,128)(2,1)S(1)}, bf16[4,64,4]{1,2,0:T(4,128)(2,1)S(1)}, u32[]{:S(2)}, u32[]{:S(2)}) collective-permute-start(bf16[4,64,4]{1,2,0:T(4,128)(2,1)S(1)} %get-tuple-element.742), channel_id=1, source_target_pairs={{0,1},{1,2},{2,3},{3,4},{4,5},{5,6},{6,7},{7,0},{8,9},{9,10},{10,1... | collective-permute-start | bytes 6152 | tf_op jit(solution)/shard_map/while/body/eval_jaxpr/ppermute | solution.py:14
  778.2 82.3 %all-gather.2.cloned.1.call-start = ((), (), s32[]{:S(2)}) async-start(), calls=%async_computation | async-start | bytes 2162688 | tf_op jit(solution)/shard_map/while/body/eval_jaxpr/all_gather | solution.py:128
  778.2 5.3 collective-permute-start
  785.4 18.1 %collective-permute-start.1 = (bf16[4,64,4]{1,2,0:T(4,128)(2,1)S(1)}, bf16[4,64,4]{1,2,0:T(4,128)(2,1)S(1)}, u32[]{:S(2)}, u32[]{:S(2)}) collective-permute-start(bf16[4,64,4]{1,2,0:T(4,128)(2,1)S(1)} %get-tuple-element.742), channel_id=1, source_target_pairs={{0,1},{1,2},{2,3},{3,4},{4,5},{5,6},{6,7},{7,0},{8,9},{9,10},{10,1... | collective-permute-start | bytes 6152 | tf_op jit(solution)/shard_map/while/body/eval_jaxpr/ppermute | solution.py:14
  930.0 82.3 %all-gather.2.cloned.1.call-start = ((), (), s32[]{:S(2)}) async-start(), calls=%async_computation | async-start | bytes 2162688 | tf_op jit(solution)/shard_map/while/body/eval_jaxpr/all_gather | solution.py:128
  930.1 5.3 collective-permute-start
  937.3 18.0 %collective-permute-start.1 = (bf16[4,64,4]{1,2,0:T(4,128)(2,1)S(1)}, bf16[4,64,4]{1,2,0:T(4,128)(2,1)S(1)}, u32[]{:S(2)}, u32[]{:S(2)}) collective-permute-start(bf16[4,64,4]{1,2,0:T(4,128)(2,1)S(1)} %get-tuple-element.742), channel_id=1, source_target_pairs={{0,1},{1,2},{2,3},{3,4},{4,5},{5,6},{6,7},{7,0},{8,9},{9,10},{10,1... | collective-permute-start | bytes 6152 | tf_op jit(solution)/shard_map/while/body/eval_jaxpr/ppermute | solution.py:14
  1081.9 82.3 %all-gather.2.cloned.1.call-start = ((), (), s32[]{:S(2)}) async-start(), calls=%async_computation | async-start | bytes 2162688 | tf_op jit(solution)/shard_map/while/body/eval_jaxpr/all_gather | solution.py:128
  1082.0 5.3 collective-permute-start
  1089.2 18.1 %collective-permute-start.1 = (bf16[4,64,4]{1,2,0:T(4,128)(2,1)S(1)}, bf16[4,64,4]{1,2,0:T(4,128)(2,1)S(1)}, u32[]{:S(2)}, u32[]{:S(2)}) collective-permute-start(bf16[4,64,4]{1,2,0:T(4,128)(2,1)S(1)} %get-tuple-element.742), channel_id=1, source_target_pairs={{0,1},{1,2},{2,3},{3,4},{4,5},{5,6},{6,7},{7,0},{8,9},{9,10},{10,1... | collective-permute-start | bytes 6152 | tf_op jit(solution)/shard_map/while/body/eval_jaxpr/ppermute | solution.py:14
  (34 other events, 635.1 us)
Sparse Core Ops, SparseCore 0:
  17.6 83.5 all-gather.1
  176.9 76.0 all-gather.1
  328.6 76.1 all-gather.1
  480.5 76.1 all-gather.1
  632.4 76.2 all-gather.1
  784.3 76.1 all-gather.1
  936.2 76.1 all-gather.1
  1088.1 76.1 all-gather.1
where the time goes:
time: 1250 us; the launch traced here: 1240 us
  blocking collectives  466 us (37%)
  local copies, waits for them, and re-layouts  348 us (28%)
  other arithmetic  200 us (16%)
  waiting for transfers between devices  147 us (12%)
  matrix products  43.5 us (3%)
  starting transfers between devices  16.1 us (1%)
  between operations  14.1 us (1%)
    all_gather x8, blocking collectives, visit_group(): lax.all_gather(visiting[1], 'blk', axis=0, tiled=True)  347 us
    reduce_max x16, other arithmetic, chamfer_direct(): jnp.max(jnp.where(key_mask[None, None, :, :], scores, NEG_FILL), axis=3)  187 us
    mul x50, local copies, waits for them, and re-layouts, dequantize(): scaled = grouped * block_scales.astype(jnp.float32)[:, :, :, None]  146 us
    mul x16, local copies, waits for them, and re-layouts, chamfer_direct(): products.reshape(query_docs, tok_count, key_docs, tok_count) * factor  129 us
    while x8, blocking collectives  119 us
    all_gather x8, waiting for transfers between devices, visit_group(): lax.all_gather(visiting[0], 'blk', axis=0, tiled=True)  104 us
    dot_general x16, matrix products, chamfer_direct(): lax.dot_general(queries, key_values.reshape(key_docs * tok_count, feature...  43.5 us
    ppermute x32, waiting for transfers between devices, from_behind(): return lax.ppermute(value, axis, pairs)  42.6 us
  transfers between devices with their start and end apart: 40, of which 24 were waited for; matrix products, arithmetic and copies ran while one was open for 2% of the time, Pallas kernels for 0%

commit v1 on v0

v1 whole, which is shorter than its diff:
```python
import functools
import math

import jax
import jax.numpy as jnp
from jax import lax
from jax.experimental import pallas as pl
from jax.experimental.pallas import tpu as pltpu
from jax.sharding import PartitionSpec as P

NEG_FILL = -1e30
MESH = pl.DeviceIdType.MESH
TORUS = (4, 4, 8)

COLS = ((0, 0, 0), (0, 0, 1), (0, 0, 7), (0, 0, 2), (0, 0, 6), (0, 0, 3), (0, 0, 5), (0, 0, 4))
ROWS = (
    (0, 0, 0), (1, 0, 0), (0, 1, 0), (3, 3, 0), (1, 3, 0),
    (2, 0, 0), (0, 2, 0), (1, 2, 0), (2, 3, 0), (2, 2, 0),
)
N_COLS = len(COLS)
N_ROWS = len(ROWS)
SLOTS = 2 * N_COLS
DOCS = 4
TOKS = 64
DIM = 128
BODY = DOCS * TOKS
BLOCK = BODY + 16


def position():
    blk = lax.axis_index("blk")
    group = lax.axis_index("group")
    return group // 2, (blk // 2) % 2 * 2 + group % 2, blk // 4, blk % 2


def device_at(x, y, z, core):
    return ((z * 2 + y // 2) * 2 + core, x * 2 + y % 2)


def shifted(offset, other=0, sign=1):
    x, y, z, core = position()
    sx, sy, sz = TORUS
    return device_at(
        (x + sign * offset[0] + sx) % sx,
        (y + sign * offset[1] + sy) % sy,
        (z + sign * offset[2] + sz) % sz,
        (core + other) % 2,
    )


def partners():
    sends = set()
    for offset in COLS:
        minus = tuple(-v % n for v, n in zip(offset, TORUS))
        for other in (0, 1):
            sends.add((offset, other))
        sends.add((minus, 0))
    for offset in ROWS:
        minus = tuple(-v % n for v, n in zip(offset, TORUS))
        sends.add((offset, 0))
        sends.add((minus, 0))
    sends.discard(((0, 0, 0), 0))
    return sorted(sends)


def lanes(shape):
    return lax.broadcasted_iota(jnp.int32, shape, len(shape) - 1)


def sublanes(shape):
    return lax.broadcasted_iota(jnp.int32, shape, len(shape) - 2)


def roll_max(value, shifts, axis):
    for shift in shifts:
        value = jnp.maximum(value, pltpu.roll(value, shift, axis))
    return value


def roll_sum(value, shifts, axis):
    for shift in shifts:
        value = value + pltpu.roll(value, shift, axis)
    return value


def prepare(quantized, scales, counts, clusters, stage, block):
    tile = (TOKS, DIM)
    spread = (lanes((4, DIM)) // 32 == sublanes((4, DIM))).astype(jnp.bfloat16)
    token = sublanes(tile)
    for doc in range(DOCS):
        scale = lax.dot_general(
            scales[doc], spread, (((0,), (0,)), ((), ())), preferred_element_type=jnp.float32
        )
        value = quantized[doc].astype(jnp.float32) * scale
        value = value.astype(jnp.bfloat16).astype(jnp.float32)
        first = jnp.broadcast_to(value[0:1], tile)
        stage[pl.ds(doc, TOKS, stride=DOCS), :] = jnp.where(token < counts[doc], value, first)
    block[0:BODY, :] = stage[...].astype(jnp.bfloat16)
    doc_of_lane = lanes((16, DIM)) % DOCS
    meta = jnp.zeros((16, DIM), jnp.int32)
    for doc in range(DOCS):
        value = jnp.where(sublanes((16, DIM)) < 8, counts[doc], clusters[doc])
        meta = jnp.where(doc_of_lane == doc, value, meta)
    block[BODY:BLOCK, :] = meta.astype(jnp.float32).astype(jnp.bfloat16)


def half_scores(rows, half, col_ref):
    first = half * 8
    best = None
    tops = []
    for tile in range(8):
        keys = [
            col_ref[first : first + 8, (2 * tile + k) * 16 : (2 * tile + k + 1) * 16, :].reshape(
                128, DIM
            )
            for k in range(2)
        ]
        scores = lax.dot_general(
            rows,
            jnp.concatenate(keys, axis=0),
            (((1,), (1,)), ((), ())),
            preferred_element_type=jnp.float32,
        )
        for k in range(2):
            part = scores[:, 128 * k : 128 * (k + 1)]
            best = part if best is None else jnp.maximum(best, part)
            tops.append(jnp.max(part.reshape(BODY // 8, 8, 128), axis=0))
    return best, tops


def kernel(
    quantized, scales, counts, clusters,
    best_ref, cluster_ref,
    stage, col_ref, row_ref, key_count, key_cluster, over_keys, tops_ref, col_best, row_out, col_out, row_in, col_in,
    col_send, col_recv, core_send, core_recv, row_send, row_recv,
    col_out_send, col_in_recv, row_out_send, row_in_recv,
):
    barrier = pltpu.get_barrier_semaphore()
    around = partners()
    for offset, other in around:
        pl.semaphore_signal(
            barrier, 1, device_id=shifted(offset, other), device_id_type=MESH
        )
    own = col_ref.at[0]
    prepare(quantized, scales, counts, clusters, stage, own)
    row_ref[0] = col_ref[0]
    pl.semaphore_wait(barrier, len(around))

    def remote(source, target, send, recv, device):
        return pltpu.make_async_remote_copy(
            src_ref=source,
            dst_ref=target,
            send_sem=send,
            recv_sem=recv,
            device_id=device,
            device_id_type=MESH,
        )

    def to_sibling(k):
        return remote(
            col_ref.at[2 * k],
            col_ref.at[2 * k + 1],
            core_send.at[k],
            core_recv.at[k],
            shifted((0, 0, 0), 1),
        )

    col_copies = [
        remote(own, col_ref.at[2 * k], col_send.at[k], col_recv.at[k], shifted(COLS[k], 0, -1))
        if k
        else None
        for k in range(N_COLS)
    ]
    row_copies = [
        remote(own, row_ref.at[r], row_send.at[r], row_recv.at[r], shifted(ROWS[r], 0, -1))
        if r
        else None
        for r in range(N_ROWS)
    ]
    core_copies = [to_sibling(k) for k in range(N_COLS)]
    for copy in reversed(col_copies[1:]):
        copy.start()
    for copy in reversed(row_copies[1:]):
        copy.start()
    core_copies[0].start()
    for k in range(1, N_COLS):
        col_copies[k].wait_recv()
        core_copies[k].start()
    for k in range(N_COLS):
        core_copies[k].wait_recv()

    small = (8, DIM)
    lane = lanes(small)
    sub = sublanes(small)
    for half in range(2):
        meta = jnp.zeros((16, DIM), jnp.float32)
        for k in range(8):
            part = col_ref[8 * half + k, BODY:BLOCK, :].astype(jnp.float32)
            meta = jnp.where(lanes((16, DIM)) // 16 == k, part, meta)
        key_count[half] = meta[0:8]
        key_cluster[half] = meta[8:16]
    col_best[...] = jnp.full(col_best.shape, NEG_FILL, jnp.float32)

    factor = 0.5 / math.sqrt(DIM)
    key_token = lane % 16 // DOCS
    same_doc = (lane % DOCS) == (sub % DOCS)

    def row_step(r, state):
        @pl.when(r > 0)
        def _():
            remote(
                row_ref.at[0], row_ref.at[r], row_send.at[r], row_recv.at[r], shifted((0, 0, 0), 1)
            ).wait_recv()

        rows = row_ref[r, 0:BODY, :]
        meta = row_ref[r, BODY:BLOCK, :].astype(jnp.float32)
        pick = lanes((16, DIM)) == sublanes((16, DIM)) % DOCS
        chosen = jnp.sum(jnp.where(pick, meta, 0.0), axis=1, keepdims=True)
        row_count = jnp.broadcast_to(chosen[0:8], small)
        row_cluster = jnp.broadcast_to(chosen[8:16], small)
        best_row = jnp.full(small, NEG_FILL, jnp.float32)
        near_row = jnp.full(small, NEG_FILL, jnp.float32)
        for half in range(2):
            best, tops = half_scores(rows, half, col_ref)
            best = roll_max(best, (DIM - 4, DIM - 8), 1)
            forward = jnp.zeros(small, jnp.float32)
            for v in range(BODY // 8):
                token = (2 * v + sub // DOCS).astype(jnp.float32)
                forward = forward + jnp.where(token < row_count, best[8 * v : 8 * v + 8], 0.0)
            forward = roll_sum(forward, (4,), 0)
            backward = jnp.zeros(small, jnp.float32)
            for t in range(TOKS // 4):
                top = roll_max(tops[t], (4,), 0)
                token = (4 * t + key_token).astype(jnp.float32)
                backward = backward + jnp.where(token < key_count[half], top, 0.0)
            backward = roll_sum(backward, (DIM - 4, DIM - 8), 1)
            chamfer = factor * (forward / row_count + backward / key_count[half])
            distinct = lane % 16 < DOCS
            if half == 0:
                distinct = distinct & ~((lane // 16 == 0) & same_doc & (r == 0))
            partner = distinct & (key_cluster[half] == row_cluster)
            overall = jnp.where(distinct, chamfer, NEG_FILL)
            within = jnp.where(partner, chamfer, NEG_FILL)
            col_best[half, 0] = jnp.maximum(col_best[half, 0], overall)
            col_best[half, 1] = jnp.maximum(col_best[half, 1], within)
            best_row = jnp.maximum(best_row, overall)
            near_row = jnp.maximum(near_row, within)

        def by_lane(value):
            top = jnp.broadcast_to(jnp.max(value, axis=1, keepdims=True), small)
            return roll_max(jnp.where(same_doc, top, NEG_FILL), (1, 2), 0)

        row_out[r] = jnp.where(sub < 4, by_lane(best_row), by_lane(near_row))
        return state

    lax.fori_loop(0, N_ROWS, row_step, 0)

    for half in range(2):
        overall = roll_max(col_best[half, 0], (4, 2, 1), 0)
        within = roll_max(col_best[half, 1], (4, 2, 1), 0)
        col_out[half] = jnp.where(sub < 4, overall, within)

    row_outs = [
        remote(
            row_out.at[r], row_in.at[r], row_out_send.at[r], row_in_recv.at[r], shifted(ROWS[r])
        )
        for r in range(1, N_ROWS)
    ]
    col_outs = [
        remote(
            col_out.at[slot // 8],
            col_in.at[slot],
            col_out_send.at[slot],
            col_in_recv.at[slot],
            shifted(COLS[slot // 2], slot % 2),
        )
        for slot in range(1, SLOTS)
    ]
    for copy in row_outs + col_outs:
        copy.start()
    for k in range(1, N_COLS):
        col_copies[k].wait_send()
    for r in range(1, N_ROWS):
        row_copies[r].wait_send()
    for k in range(N_COLS):
        core_copies[k].wait_send()
    for copy in row_outs + col_outs:
        copy.wait_send()

    total = jnp.where(lane // 16 == 0, col_out[0], NEG_FILL)
    for slot in range(1, SLOTS):
        col_outs[slot - 1].wait_recv()
        total = jnp.maximum(total, jnp.where(lane // 16 == slot % 8, col_in[slot], NEG_FILL))
    total = roll_max(total, (16, 32, 64), 1)
    total = jnp.maximum(total, row_out[0])
    for r in range(1, N_ROWS):
        row_outs[r - 1].wait_recv()
        total = jnp.maximum(total, row_in[r])
    best_ref[...] = total[0:1, 0:DOCS]
    cluster_ref[...] = total[4:5, 0:DOCS]


def shards(quantized, block_scales, token_counts, cluster_ids):
    vmem = pl.BlockSpec(memory_space=pltpu.VMEM)
    smem = pl.BlockSpec(memory_space=pltpu.SMEM)
    scores = pl.pallas_call(
        kernel,
        out_shape=(
            jax.ShapeDtypeStruct((1, DOCS), jnp.float32),
            jax.ShapeDtypeStruct((1, DOCS), jnp.float32),
        ),
        in_specs=[vmem, vmem, smem, smem],
        out_specs=(vmem, vmem),
        scratch_shapes=[
            pltpu.VMEM((BODY, DIM), jnp.float32),
            pltpu.VMEM((SLOTS, BLOCK, DIM), jnp.bfloat16),
            pltpu.VMEM((N_ROWS, BLOCK, DIM), jnp.bfloat16),
            pltpu.VMEM((2, 8, DIM), jnp.float32),
            pltpu.VMEM((2, 8, DIM), jnp.float32),
            pltpu.VMEM((BODY, DIM), jnp.float32),
            pltpu.VMEM((TOKS // 4, 8, DIM), jnp.float32),
            pltpu.VMEM((2, 2, 8, DIM), jnp.float32),
            pltpu.VMEM((N_ROWS, 8, DIM), jnp.float32),
            pltpu.VMEM((2, 8, DIM), jnp.float32),
            pltpu.VMEM((N_ROWS, 8, DIM), jnp.float32),
            pltpu.VMEM((SLOTS, 8, DIM), jnp.float32),
            pltpu.SemaphoreType.DMA((N_COLS,)),
            pltpu.SemaphoreType.DMA((N_COLS,)),
            pltpu.SemaphoreType.DMA((N_COLS,)),
            pltpu.SemaphoreType.DMA((N_COLS,)),
            pltpu.SemaphoreType.DMA((N_ROWS,)),
            pltpu.SemaphoreType.DMA((N_ROWS,)),
            pltpu.SemaphoreType.DMA((SLOTS,)),
            pltpu.SemaphoreType.DMA((SLOTS,)),
            pltpu.SemaphoreType.DMA((N_ROWS,)),
            pltpu.SemaphoreType.DMA((N_ROWS,)),
        ],
        compiler_params=pltpu.CompilerParams(
            collective_id=0, has_side_effects=True, vmem_limit_bytes=40 << 20
        ),
    )(quantized, jnp.swapaxes(block_scales, 1, 2), token_counts, cluster_ids)
    return scores[0].reshape(DOCS), scores[1].reshape(DOCS)


def solution(mesh):
    placed = (
        P(("blk", "group"), None, None),
        P(("blk", "group"), None, None),
        P(("blk", "group")),
        P(("blk", "group")),
    )
    return jax.shard_map(
        shards,
        mesh=mesh,
        in_specs=placed,
        out_specs=(P(("blk", "group")), P(("blk", "group"))),
        check_vma=False,
    )
```

time: 1250 us -> 46.1 us (0.04)
  blocking collectives: 466 us -> 0 us
  local copies, waits for them, and re-layouts: 348 us -> 3.21 us
  other arithmetic: 200 us -> 0 us
  waiting for transfers between devices: 147 us -> 0 us
  matrix products: 43.5 us -> 0 us
  Pallas kernels: 0 us -> 42.1 us
  starting transfers between devices: 16.1 us -> 0 us
  between operations: 14.1 us -> 0.66 us
    all_gather x8 -> x0, blocking collectives: 347 us -> none  [visit_group(): lax.all_gather(visiting[1], 'blk', axis=0, tiled=True)]
    mul x66 -> x0, local copies, waits for them, and re-layouts: 275 us -> none  [the longest x50 146 us: dequantize(): scaled = grouped * block_scales.astype(jnp.float32)[:, :, :, None]]
    reduce_max x24 -> x0, other arithmetic: 188 us -> none  [the longest x16 187 us: chamfer_direct(): jnp.max(jnp.where(key_mask[None, None, :, :], scores, NEG_FILL), axis=3)]
    while x8 -> x0, blocking collectives: 119 us -> none
    all_gather x8 -> x0, waiting for transfers between devices: 104 us -> none  [visit_group(): lax.all_gather(visiting[0], 'blk', axis=0, tiled=True)]
    dot_general x16 -> x0, matrix products: 43.5 us -> none  [chamfer_direct(): lax.dot_general(queries, key_values.reshape(key_docs * tok_count, feature...]
    ppermute x32 -> x0, waiting for transfers between devices: 42.6 us -> none  [from_behind(): return lax.ppermute(value, axis, pairs)]
    pallas_call x0 -> x1, Pallas kernels: none -> 42.1 us  [shards(): pl.pallas_call(kernel, out_shape=(jax.ShapeDtypeStruct((1, DOCS), jnp.flo...]
  transfers between devices with their start and end apart: 40 -> 0, of which waited for: 24 -> 0; matrix products, arithmetic and copies ran while one was open for 2% -> 0% of each run, Pallas kernels for 0% -> 0%
where the time goes in v1:
time: 46.1 us; the launch traced here: 46 us
  Pallas kernels  42.1 us (91%)
  local copies, waits for them, and re-layouts  3.21 us (7%)
  between operations  0.66 us (1%)
    pallas_call x1, Pallas kernels, shards(): pl.pallas_call(kernel, out_shape=(jax.ShapeDtypeStruct((1, DOCS), jnp.flo...  42.1 us
    unnamed x10, local copies, waits for them, and re-layouts  3.21 us

profile of v1, /device:TPU:1, one launch (start us, length us, event | category | flops | bytes accessed | tf_op | source)
XLA Modules:
  0.0 46.0 jit_solution(16657248764238959412)
XLA Ops:
  0.6 0.0 copy-start.3
  0.6 0.0 copy-start.2
  0.7 0.6 %copy-done.3 = s32[4]{0:T(128)S(1)} copy-done((s32[4]{0:T(128)S(1)}, s32[4]{0:T(128)}, u32[]{:S(2)}) %copy-start.3) | copy-done | bytes 40
  1.3 0.0 copy-done.2
  1.3 0.0 copy-start
  1.3 0.8 %copy-done = bf16[4,64,128]{2,1,0:T(8,128)(2,1)S(1)} copy-done((bf16[4,64,128]{2,1,0:T(8,128)(2,1)S(1)}, bf16[4,64,128]{2,1,0:T(8,128)(2,1)}, u32[]{:S(2)}) %copy-start) | copy-done | bytes 65560
  2.1 0.0 copy-start.1
  2.1 0.7 %copy-done.1 = bf16[4,64,4]{1,2,0:T(4,128)(2,1)S(1)} copy-done((bf16[4,64,4]{1,2,0:T(4,128)(2,1)S(1)}, bf16[4,64,4]{1,2,0:T(4,128)(2,1)}, u32[]{:S(2)}) %copy-start.1) | copy-done | bytes 2072
  2.8 42.1 %shard_map.59 = (f32[1,4]{1,0:T(1,128)S(1)}, f32[1,4]{1,0:T(1,128)S(1)}) custom-call(bf16[4,64,128]{2,1,0:T(8,128)(2,1)S(1)} %copy-done, bf16[4,4,64]{2,1,0:T(4,128)(2,1)S(1)} %bitcast.3, s32[4]{0:T(128)S(1)} %copy-done.2, s32[4]{0:T(128)S(1)} %copy-done.3), custom_call_target="tpu_custom_call" | custom-call | tf_op jit(solution)/shard_map/pallas_call | solution.py:306
  44.9 0.5 %copy.8 = f32[4]{0:T(128)} copy(f32[4]{0:T(128)S(1)} %bitcast.5) | data formatting | bytes 32
  45.5 0.5 %copy.9 = f32[4]{0:T(128)} copy(f32[4]{0:T(128)S(1)} %bitcast.4) | data formatting | bytes 32
Async XLA Ops:
  0.6 0.7 %copy-start.3 = (s32[4]{0:T(128)S(1)}, s32[4]{0:T(128)}, u32[]{:S(2)}) copy-start(s32[4]{0:T(128)} %clusters.1) | copy-start | bytes 52
  0.6 0.7 %copy-start.2 = (s32[4]{0:T(128)S(1)}, s32[4]{0:T(128)}, u32[]{:S(2)}) copy-start(s32[4]{0:T(128)} %counts.1) | copy-start | bytes 52
  1.3 0.8 %copy-start = (bf16[4,64,128]{2,1,0:T(8,128)(2,1)S(1)}, bf16[4,64,128]{2,1,0:T(8,128)(2,1)}, u32[]{:S(2)}) copy-start(bf16[4,64,128]{2,1,0:T(8,128)(2,1)} %quantized.1) | copy-start | bytes 196612
  2.1 0.7 %copy-start.1 = (bf16[4,64,4]{1,2,0:T(4,128)(2,1)S(1)}, bf16[4,64,4]{1,2,0:T(4,128)(2,1)}, u32[]{:S(2)}) copy-start(bf16[4,64,4]{1,2,0:T(4,128)(2,1)} %param.5) | copy-start | bytes 6148

commit v2 on v1

v2 whole, which is shorter than its diff:
```python
import functools
import math

import jax
import jax.numpy as jnp
from jax import lax
from jax.experimental import pallas as pl
from jax.experimental.pallas import tpu as pltpu
from jax.sharding import PartitionSpec as P

NEG_FILL = -1e30
MESH = pl.DeviceIdType.MESH
TORUS = (4, 4, 8)

COLS = ((0, 0, 0), (0, 0, 1), (0, 0, 7), (0, 0, 2), (0, 0, 6), (0, 0, 3), (0, 0, 5), (0, 0, 4))
ROWS = (
    (0, 0, 0), (1, 0, 0), (0, 1, 0), (3, 3, 0), (3, 1, 0),
    (2, 0, 0), (0, 2, 0), (1, 2, 0), (2, 3, 0), (2, 2, 0),
)
N_COLS = len(COLS)
N_ROWS = len(ROWS)
SLOTS = 2 * N_COLS
DOCS = 4
TOKS = 64
DIM = 128
BODY = DOCS * TOKS
BLOCK = BODY + 16
CUT = 144
EARLY = 3


def position():
    blk = lax.axis_index("blk")
    group = lax.axis_index("group")
    return group >> 1, (blk & 2) | (group & 1), blk >> 2, blk & 1


def device_at(x, y, z, core):
    return ((z << 2) | (y & 2) | core, (x << 1) | (y & 1))


def shifted(offset, other=0, sign=1):
    x, y, z, core = position()
    step = tuple(sign * v % n for v, n in zip(offset, TORUS))
    return device_at(
        (x + step[0]) & (TORUS[0] - 1) if step[0] else x,
        (y + step[1]) & (TORUS[1] - 1) if step[1] else y,
        (z + step[2]) & (TORUS[2] - 1) if step[2] else z,
        core ^ other if other else core,
    )


def partners():
    sends = set()
    for offset in COLS:
        minus = tuple(-v % n for v, n in zip(offset, TORUS))
        for other in (0, 1):
            sends.add((offset, other))
        sends.add((minus, 0))
    for offset in ROWS:
        minus = tuple(-v % n for v, n in zip(offset, TORUS))
        sends.add((offset, 0))
        sends.add((minus, 0))
    sends.discard(((0, 0, 0), 0))
    return sorted(sends)


def lanes(shape):
    return lax.broadcasted_iota(jnp.int32, shape, len(shape) - 1)


def sublanes(shape):
    return lax.broadcasted_iota(jnp.int32, shape, len(shape) - 2)


def roll_max(value, shifts, axis):
    for shift in shifts:
        value = jnp.maximum(value, pltpu.roll(value, shift, axis))
    return value


def roll_sum(value, shifts, axis):
    for shift in shifts:
        value = value + pltpu.roll(value, shift, axis)
    return value


def prepare(quantized, scales, counts, clusters, stage, block):
    tile = (TOKS, DIM)
    spread = (lanes((4, DIM)) // 32 == sublanes((4, DIM))).astype(jnp.bfloat16)
    token = sublanes(tile)
    for doc in range(DOCS):
        scale = lax.dot_general(
            scales[doc], spread, (((0,), (0,)), ((), ())), preferred_element_type=jnp.float32
        )
        value = quantized[doc].astype(jnp.float32) * scale
        value = value.astype(jnp.bfloat16).astype(jnp.float32)
        first = jnp.broadcast_to(value[0:1], tile)
        stage[pl.ds(doc, TOKS, stride=DOCS), :] = jnp.where(token < counts[doc], value, first)
    block[0:BODY, :] = stage[...].astype(jnp.bfloat16)
    doc_of_lane = lanes((16, DIM)) % DOCS
    meta = jnp.zeros((16, DIM), jnp.int32)
    for doc in range(DOCS):
        value = jnp.where(sublanes((16, DIM)) < 8, counts[doc], clusters[doc])
        meta = jnp.where(doc_of_lane == doc, value, meta)
    block[BODY:BLOCK, :] = meta.astype(jnp.float32).astype(jnp.bfloat16)


def half_scores(rows, half, col_ref):
    first = half * 8
    blocks = rows.shape[0] // BODY
    best = None
    tops = [[] for _ in range(blocks)]
    for tile in range(8):
        keys = [
            col_ref[first : first + 8, (2 * tile + k) * 16 : (2 * tile + k + 1) * 16, :].reshape(
                128, DIM
            )
            for k in range(2)
        ]
        scores = lax.dot_general(
            rows,
            jnp.concatenate(keys, axis=0),
            (((1,), (1,)), ((), ())),
            preferred_element_type=jnp.float32,
        )
        for k in range(2):
            part = scores[:, 128 * k : 128 * (k + 1)]
            best = part if best is None else jnp.maximum(best, part)
            for q in range(blocks):
                block = part[BODY * q : BODY * (q + 1)]
                tops[q].append(jnp.max(block.reshape(BODY // 8, 8, 128), axis=0))
    return [best[BODY * q : BODY * (q + 1)] for q in range(blocks)], tops


def row_owner(r):
    x, y, z, core = position()
    xs = sum(offset[0] * 4**k for k, offset in enumerate(ROWS))
    ys = sum(offset[1] * 4**k for k, offset in enumerate(ROWS))
    return device_at((x + (xs >> (2 * r))) & 3, (y + (ys >> (2 * r))) & 3, z, core)


def kernel(
    quantized_hbm, scales_hbm, counts_hbm, clusters_hbm,
    best_ref, cluster_ref,
    quantized, scales, counts, clusters, load_sem,
    stage, col_ref, row_ref, key_count, key_cluster, row_side, row_best, col_best, row_out, col_out, row_in, col_in,
    col_send, col_recv, core_send, core_recv, row_send, row_recv,
    col_out_send, col_in_recv, row_out_send, row_in_recv,
):
    loads = [
        pltpu.make_async_copy(source, target, load_sem.at[k])
        for k, (source, target) in enumerate(
            (
                (counts_hbm, counts),
                (clusters_hbm, clusters),
                (scales_hbm, scales),
                (quantized_hbm, quantized),
            )
        )
    ]
    for load in loads:
        load.start()
    barrier = pltpu.get_barrier_semaphore()
    around = partners()
    for offset, other in around:
        pl.semaphore_signal(barrier, 1, device_id=shifted(offset, other), device_id_type=MESH)
    for load in loads:
        load.wait()
    own = col_ref.at[0]
    prepare(quantized, scales, counts, clusters, stage, own)
    row_ref[0] = col_ref[0]
    col_best[...] = jnp.full(col_best.shape, NEG_FILL, jnp.float32)
    pl.semaphore_wait(barrier, len(around))

    def remote(source, target, send, recv, device):
        return pltpu.make_async_remote_copy(
            src_ref=source,
            dst_ref=target,
            send_sem=send,
            recv_sem=recv,
            device_id=device,
            device_id_type=MESH,
        )

    def along(k, source, target, part, device):
        source, target = col_ref.at[2 * source], col_ref.at[2 * target]
        if part is not None:
            source, target = source.at[part[0] : part[1]], target.at[part[0] : part[1]]
        return remote(source, target, col_send.at[k], col_recv.at[k], device)

    col_copies = [
        along(0, 4, 7, (CUT, BLOCK), shifted(COLS[3])),
        along(1, 0, 1, None, shifted(COLS[2])),
        along(2, 0, 2, None, shifted(COLS[1])),
        along(3, 0, 3, None, shifted(COLS[4])),
        along(4, 0, 4, None, shifted(COLS[3])),
        along(5, 3, 5, None, shifted(COLS[2])),
        along(6, 4, 6, None, shifted(COLS[1])),
        along(7, 3, 7, (0, CUT), shifted(COLS[4])),
    ]
    core_copies = [
        remote(
            col_ref.at[2 * k],
            col_ref.at[2 * k + 1],
            core_send.at[k],
            core_recv.at[k],
            shifted((0, 0, 0), 1),
        )
        for k in range(N_COLS)
    ]
    row_copies = [
        remote(own, row_ref.at[r], row_send.at[r], row_recv.at[r], shifted(ROWS[r], 0, -1))
        for r in range(1, N_ROWS)
    ]
    for k in (3, 4, 1, 2):
        col_copies[k].start()
    core_copies[0].start()
    row_waves = ((1, 2, 3), (4, 5, 6), (7, 8, 9))
    for k, wave in enumerate(row_waves):
        for r in row_waves[k - 1] if k else ():
            row_copies[r - 1].wait_send()
        for r in wave:
            row_copies[r - 1].start()
    col_copies[3].wait_recv()
    col_copies[5].start()
    col_copies[7].start()
    col_copies[4].wait_recv()
    col_copies[6].start()
    col_copies[0].start()
    core_copies[3].start()
    for k in (1, 2):
        col_copies[k].wait_recv()
        core_copies[k].start()
    core_copies[4].start()

    small = (8, DIM)
    lane = lanes(small)
    sub = sublanes(small)
    factor = 0.5 / math.sqrt(DIM)
    same_doc = (lane % DOCS) == (sub % DOCS)

    def read_meta(half):
        for k in range(4 * half, 4 * half + 4):
            core_copies[k].wait_recv()
        meta = jnp.zeros((16, DIM), jnp.float32)
        for k in range(8):
            part = col_ref[8 * half + k, BODY:BLOCK, :].astype(jnp.float32)
            meta = jnp.where(lanes((16, DIM)) // 16 == k, part, meta)
        key_count[half] = meta[0:8]
        key_cluster[half] = meta[8:16]

    def row_meta(r):
        meta = row_ref[r, BODY:BLOCK, :].astype(jnp.float32)
        pick = lanes((16, DIM)) == sublanes((16, DIM)) % DOCS
        chosen = jnp.sum(jnp.where(pick, meta, 0.0), axis=1, keepdims=True)
        row_side[r, 0] = jnp.broadcast_to(chosen[0:8], small)
        row_side[r, 1] = jnp.broadcast_to(chosen[8:16], small)

    def pair_unit(p, half):
        rows = row_ref[pl.ds(2 * p, 2), 0:BODY, :].reshape(2 * BODY, DIM)
        bests, all_tops = half_scores(rows, half, col_ref)
        found = []
        for q in range(2):
            r = 2 * p + q
            row_count, row_cluster = row_side[r, 0], row_side[r, 1]
            best = roll_max(bests[q], (DIM - 4, DIM - 8), 1)
            forward = roll_sum(jnp.sum(best.reshape(BODY // 8, 8, DIM), axis=0), (4,), 0)
            start = jnp.where(sub < 4, best[0:8], pltpu.roll(best[0:8], 4, 0))
            forward = forward - (TOKS - row_count) * start
            tops = [roll_max(top, (4,), 0) for top in all_tops[q]]
            backward = roll_sum(functools.reduce(jnp.add, tops), (DIM - 4, DIM - 8), 1)
            backward = backward - (TOKS - key_count[half]) * tops[0]
            chamfer = factor * (forward / row_count + backward / key_count[half])
            distinct = lane % 16 < DOCS
            if half == 0:
                distinct = distinct & ~((lane // 16 == 0) & same_doc & (r == 0))
            partner = distinct & (key_cluster[half] == row_cluster)
            found.append((jnp.where(distinct, chamfer, NEG_FILL), jnp.where(partner, chamfer, NEG_FILL)))
        for side in range(2):
            top = jnp.maximum(found[0][side], found[1][side])
            col_best[half, side] = jnp.maximum(col_best[half, side], top)
        return found

    def row_copy(r):
        return remote(row_ref.at[0], row_ref.at[r], row_send.at[r], row_recv.at[r], row_owner(r))

    def row_result(r):
        return remote(
            row_out.at[r], row_in.at[r], row_out_send.at[r], row_in_recv.at[r], row_owner(r)
        )

    def first_half(p, state):
        @pl.when(p > 0)
        def _():
            row_copy(2 * p).wait_recv()

        row_copy(2 * p + 1).wait_recv()
        for q in range(2):
            row_meta(2 * p + q)
        for q, found in enumerate(pair_unit(p, 0)):
            row_best[2 * p + q, 0] = found[0]
            row_best[2 * p + q, 1] = found[1]
        return state

    def by_lane(value):
        top = jnp.broadcast_to(jnp.max(value, axis=1, keepdims=True), small)
        return roll_max(jnp.where(same_doc, top, NEG_FILL), (1, 2), 0)

    def second_half(p, state):
        for q, (overall, within) in enumerate(pair_unit(p, 1)):
            r = 2 * p + q
            overall = by_lane(jnp.maximum(overall, row_best[r, 0]))
            within = by_lane(jnp.maximum(within, row_best[r, 1]))
            row_out[r] = jnp.where(sub < 4, overall, within)

        @pl.when(p > 0)
        def _():
            row_result(2 * p).start()

        row_result(2 * p + 1).start()
        return state

    col_outs = [
        remote(
            col_out.at[slot // 8],
            col_in.at[slot],
            col_out_send.at[slot],
            col_in_recv.at[slot],
            shifted(COLS[slot // 2], slot % 2),
        )
        for slot in range(SLOTS)
    ]

    def return_cols(half):
        overall = roll_max(col_best[half, 0], (4, 2, 1), 0)
        within = roll_max(col_best[half, 1], (4, 2, 1), 0)
        col_out[half] = jnp.where(sub < 4, overall, within)
        for slot in range(max(1, 8 * half), 8 * half + 8):
            col_outs[slot].start()

    read_meta(0)
    lax.fori_loop(0, EARLY, first_half, 0)
    for k in (5, 6):
        col_copies[k].wait_recv()
        core_copies[k].start()
    col_copies[7].wait_recv()
    col_copies[0].wait_recv()
    core_copies[7].start()
    lax.fori_loop(EARLY, N_ROWS // 2, first_half, 0)
    return_cols(0)
    read_meta(1)
    lax.fori_loop(0, N_ROWS // 2, second_half, 0)
    return_cols(1)

    for copy in col_copies + [row_copies[r - 1] for r in row_waves[-1]] + core_copies:
        copy.wait_send()
    total = jnp.where(lane // 16 == 0, col_out[0], NEG_FILL)
    for slot in range(1, SLOTS):
        col_outs[slot].wait_recv()
        total = jnp.maximum(total, jnp.where(lane // 16 == slot % 8, col_in[slot], NEG_FILL))
    total = roll_max(total, (16, 32, 64), 1)
    total = jnp.maximum(total, row_out[0])
    for r in range(1, N_ROWS):
        row_result(r).wait_recv()
        total = jnp.maximum(total, row_in[r])
    best_ref[...] = total[0:1, 0:DOCS]
    cluster_ref[...] = total[4:5, 0:DOCS]
    for slot in range(1, SLOTS):
        col_outs[slot].wait_send()
    for r in range(1, N_ROWS):
        row_result(r).wait_send()


def shards(quantized, block_scales, token_counts, cluster_ids):
    vmem = pl.BlockSpec(memory_space=pltpu.VMEM)
    hbm = pl.BlockSpec(memory_space=pltpu.HBM)
    scores = pl.pallas_call(
        kernel,
        out_shape=(
            jax.ShapeDtypeStruct((1, DOCS), jnp.float32),
            jax.ShapeDtypeStruct((1, DOCS), jnp.float32),
        ),
        in_specs=[hbm] * 4,
        out_specs=(vmem, vmem),
        scratch_shapes=[
            pltpu.VMEM((DOCS, TOKS, DIM), jnp.bfloat16),
            pltpu.VMEM((DOCS, 4, TOKS), jnp.bfloat16),
            pltpu.SMEM((DOCS,), jnp.int32),
            pltpu.SMEM((DOCS,), jnp.int32),
            pltpu.SemaphoreType.DMA((4,)),
            pltpu.VMEM((BODY, DIM), jnp.float32),
            pltpu.VMEM((SLOTS, BLOCK, DIM), jnp.bfloat16),
            pltpu.VMEM((N_ROWS, BLOCK, DIM), jnp.bfloat16),
            pltpu.VMEM((2, 8, DIM), jnp.float32),
            pltpu.VMEM((2, 8, DIM), jnp.float32),
            pltpu.VMEM((N_ROWS, 2, 8, DIM), jnp.float32),
            pltpu.VMEM((N_ROWS, 2, 8, DIM), jnp.float32),
            pltpu.VMEM((2, 2, 8, DIM), jnp.float32),
            pltpu.VMEM((N_ROWS, 8, DIM), jnp.float32),
            pltpu.VMEM((2, 8, DIM), jnp.float32),
            pltpu.VMEM((N_ROWS, 8, DIM), jnp.float32),
            pltpu.VMEM((SLOTS, 8, DIM), jnp.float32),
            pltpu.SemaphoreType.DMA((N_COLS,)),
            pltpu.SemaphoreType.DMA((N_COLS,)),
            pltpu.SemaphoreType.DMA((N_COLS,)),
            pltpu.SemaphoreType.DMA((N_COLS,)),
            pltpu.SemaphoreType.DMA((N_ROWS,)),
            pltpu.SemaphoreType.DMA((N_ROWS,)),
            pltpu.SemaphoreType.DMA((SLOTS,)),
            pltpu.SemaphoreType.DMA((SLOTS,)),
            pltpu.SemaphoreType.DMA((N_ROWS,)),
            pltpu.SemaphoreType.DMA((N_ROWS,)),
        ],
        compiler_params=pltpu.CompilerParams(
            collective_id=0, has_side_effects=True, vmem_limit_bytes=63 << 20
        ),
    )(quantized, jnp.swapaxes(block_scales, 1, 2), token_counts, cluster_ids)
    return scores[0].reshape(DOCS), scores[1].reshape(DOCS)


def solution(mesh):
    placed = (
        P(("blk", "group"), None, None),
        P(("blk", "group"), None, None),
        P(("blk", "group")),
        P(("blk", "group")),
    )
    return jax.shard_map(
        shards,
        mesh=mesh,
        in_specs=placed,
        out_specs=(P(("blk", "group")), P(("blk", "group"))),
        check_vma=False,
    )
```

time: 46.1 us -> 37.8 us (0.82)
  Pallas kernels: 42.1 us -> 35.2 us
  local copies, waits for them, and re-layouts: 3.21 us -> 1.8 us
    pallas_call x1, Pallas kernels: 42.1 us -> 35.2 us  [shards(): pl.pallas_call(kernel, out_shape=(jax.ShapeDtypeStruct((1, DOCS), jnp.flo...]
    unnamed x10 -> x6, local copies, waits for them, and re-layouts: 3.21 us -> 1.8 us
where the time goes in v2:
time: 37.8 us; the launch traced here: 37.6 us
  Pallas kernels  35.2 us (93%)
  local copies, waits for them, and re-layouts  1.8 us (5%)
  between operations  0.65 us (2%)
    pallas_call x1, Pallas kernels, shards(): pl.pallas_call(kernel, out_shape=(jax.ShapeDtypeStruct((1, DOCS), jnp.flo...  35.2 us
    unnamed x6, local copies, waits for them, and re-layouts  1.8 us

profile of v2, /device:TPU:1, one launch (start us, length us, event | category | flops | bytes accessed | tf_op | source)
XLA Modules:
  0.0 37.6 jit_solution(4366748654361684327)
XLA Ops:
  0.6 35.2 %shard_map.59 = (f32[1,4]{1,0:T(1,128)}, f32[1,4]{1,0:T(1,128)}) custom-call(bf16[4,64,128]{2,1,0:T(8,128)(2,1)} %quantized_hbm.1, bf16[4,4,64]{2,1,0:T(4,128)(2,1)} %bitcast.3, s32[4]{0:T(128)} %counts_hbm.1, s32[4]{0:T(128)} %clusters_hbm.1), custom_call_target="tpu_custom_call" | custom-call | tf_op jit(solution)/shard_map/pallas_call | solution.py:378
  35.8 0.0 copy-start.1
  35.8 0.7 %copy-done.1 = f32[1,4]{1,0:T(1,128)S(1)} copy-done((f32[1,4]{1,0:T(1,128)S(1)}, f32[1,4]{1,0:T(1,128)}, u32[]{:S(2)}) %copy-start.1) | copy-done | bytes 40
  36.5 0.0 copy-start
  36.5 0.5 %copy.8 = f32[4]{0:T(128)} copy(f32[4]{0:T(128)S(1)} %bitcast.5) | data formatting | bytes 32
  37.0 0.1 copy-done
  37.1 0.5 %copy.9 = f32[4]{0:T(128)} copy(f32[4]{0:T(128)S(1)} %bitcast.4) | data formatting | bytes 32
Async XLA Ops:
  35.8 0.7 %copy-start.1 = (f32[1,4]{1,0:T(1,128)S(1)}, f32[1,4]{1,0:T(1,128)}, u32[]{:S(2)}) copy-start(f32[1,4]{1,0:T(1,128)} %get-tuple-element.4) | copy-start | bytes 52
  36.5 0.6 %copy-start = (f32[1,4]{1,0:T(1,128)S(1)}, f32[1,4]{1,0:T(1,128)}, u32[]{:S(2)}) copy-start(f32[1,4]{1,0:T(1,128)} %get-tuple-element.5) | copy-start | bytes 52

commit v3 on v2

--- a/solution.py
+++ b/solution.py
@@ -26,7 +26,7 @@
 BODY = DOCS * TOKS
 BLOCK = BODY + 16
 CUT = 144
-EARLY = 3
+EARLY = 4
 
 
 def position():
@@ -142,7 +142,7 @@
 
 def kernel(
     quantized_hbm, scales_hbm, counts_hbm, clusters_hbm,
-    best_ref, cluster_ref,
+    best_ref,
     quantized, scales, counts, clusters, load_sem,
     stage, col_ref, row_ref, key_count, key_cluster, row_side, row_best, col_best, row_out, col_out, row_in, col_in,
     col_send, col_recv, core_send, core_recv, row_send, row_recv,
@@ -314,11 +314,6 @@
             within = by_lane(jnp.maximum(within, row_best[r, 1]))
             row_out[r] = jnp.where(sub < 4, overall, within)
 
-        @pl.when(p > 0)
-        def _():
-            row_result(2 * p).start()
-
-        row_result(2 * p + 1).start()
         return state
 
     col_outs = [
@@ -336,7 +331,7 @@
         overall = roll_max(col_best[half, 0], (4, 2, 1), 0)
         within = roll_max(col_best[half, 1], (4, 2, 1), 0)
         col_out[half] = jnp.where(sub < 4, overall, within)
-        for slot in range(max(1, 8 * half), 8 * half + 8):
+        for slot in reversed(range(max(1, 8 * half), 8 * half + 8)):
             col_outs[slot].start()
 
     read_meta(0)
@@ -350,8 +345,10 @@
     lax.fori_loop(EARLY, N_ROWS // 2, first_half, 0)
     return_cols(0)
     read_meta(1)
-    lax.fori_loop(0, N_ROWS // 2, second_half, 0)
+    lax.fori_loop(0, N_ROWS // 2, second_half, 0, unroll=True)
     return_cols(1)
+    for r in reversed(range(1, N_ROWS)):
+        row_result(r).start()
 
     for copy in col_copies + [row_copies[r - 1] for r in row_waves[-1]] + core_copies:
         copy.wait_send()
@@ -364,8 +361,7 @@
     for r in range(1, N_ROWS):
         row_result(r).wait_recv()
         total = jnp.maximum(total, row_in[r])
-    best_ref[...] = total[0:1, 0:DOCS]
-    cluster_ref[...] = total[4:5, 0:DOCS]
+    best_ref[...] = total
     for slot in range(1, SLOTS):
         col_outs[slot].wait_send()
     for r in range(1, N_ROWS):
@@ -377,12 +373,9 @@
     hbm = pl.BlockSpec(memory_space=pltpu.HBM)
     scores = pl.pallas_call(
         kernel,
-        out_shape=(
-            jax.ShapeDtypeStruct((1, DOCS), jnp.float32),
-            jax.ShapeDtypeStruct((1, DOCS), jnp.float32),
-        ),
+        out_shape=jax.ShapeDtypeStruct((8, DIM), jnp.float32),
         in_specs=[hbm] * 4,
-        out_specs=(vmem, vmem),
+        out_specs=vmem,
         scratch_shapes=[
             pltpu.VMEM((DOCS, TOKS, DIM), jnp.bfloat16),
             pltpu.VMEM((DOCS, 4, TOKS), jnp.bfloat16),
@@ -416,7 +409,7 @@
             collective_id=0, has_side_effects=True, vmem_limit_bytes=63 << 20
         ),
     )(quantized, jnp.swapaxes(block_scales, 1, 2), token_counts, cluster_ids)
-    return scores[0].reshape(DOCS), scores[1].reshape(DOCS)
+    return scores[0, :DOCS], scores[4, :DOCS]
 
 
 def solution(mesh):

time: 37.8 us -> 35.1 us (0.929)
  Pallas kernels: 35.2 us -> 32.9 us
  local copies, waits for them, and re-layouts: 1.8 us -> 1.26 us
    pallas_call x1, Pallas kernels: 35.2 us -> 32.9 us  [shards(): pl.pallas_call(kernel, out_shape=jax.ShapeDtypeStruct((8, DIM), jnp.float...]
    unnamed x6 -> x0, local copies, waits for them, and re-layouts: 1.8 us -> none
    squeeze x0 -> x1, local copies, waits for them, and re-layouts: none -> 1.26 us  [shards(): return (scores[0, :DOCS], scores[4, :DOCS])]
where the time goes in v3:
time: 35.1 us; the launch traced here: 34.8 us
  Pallas kernels  32.9 us (94%)
  local copies, waits for them, and re-layouts  1.26 us (4%)
  between operations  0.64 us (2%)
    pallas_call x1, Pallas kernels, shards(): pl.pallas_call(kernel, out_shape=jax.ShapeDtypeStruct((8, DIM), jnp.float...  32.9 us
    squeeze x1, local copies, waits for them, and re-layouts, shards(): return (scores[0, :DOCS], scores[4, :DOCS])  1.26 us

profile of v3, /device:TPU:1, one launch (start us, length us, event | category | flops | bytes accessed | tf_op | source)
XLA Modules:
  0.0 34.8 jit_solution(15393644075839225541)
XLA Ops:
  0.6 32.9 %shard_map.59 = f32[8,128]{1,0:T(8,128)} custom-call(bf16[4,64,128]{2,1,0:T(8,128)(2,1)} %quantized_hbm.1, bf16[4,4,64]{2,1,0:T(4,128)(2,1)} %bitcast.5, s32[4]{0:T(128)} %counts_hbm.1, s32[4]{0:T(128)} %clusters_hbm.1), custom_call_target="tpu_custom_call" | custom-call | tf_op jit(solution)/shard_map/pallas_call | solution.py:374
  33.5 1.3 %slice_bitcast_fusion = (f32[4]{0:T(128)}, f32[4]{0:T(128)}) fusion(f32[8,128]{1,0:T(8,128)} %shard_map.59), kind=kLoop, calls=%fused_computation | loop fusion | bytes 64 | tf_op jit(solution)/shard_map/squeeze | solution.py:412

commit v4 on v3

--- a/solution.py
+++ b/solution.py
@@ -14,9 +14,10 @@
 
 COLS = ((0, 0, 0), (0, 0, 1), (0, 0, 7), (0, 0, 2), (0, 0, 6), (0, 0, 3), (0, 0, 5), (0, 0, 4))
 ROWS = (
-    (0, 0, 0), (1, 0, 0), (0, 1, 0), (3, 3, 0), (3, 1, 0),
-    (2, 0, 0), (0, 2, 0), (1, 2, 0), (2, 3, 0), (2, 2, 0),
+    (0, 0, 0), (2, 0, 0), (1, 0, 0), (0, 1, 0), (3, 3, 0),
+    (3, 1, 0), (1, 2, 0), (2, 3, 0), (0, 2, 0), (2, 2, 0),
 )
+FOLDED = (0, 4)
 N_COLS = len(COLS)
 N_ROWS = len(ROWS)
 SLOTS = 2 * N_COLS
@@ -26,7 +27,6 @@
 BODY = DOCS * TOKS
 BLOCK = BODY + 16
 CUT = 144
-EARLY = 4
 
 
 def position():
@@ -106,17 +106,23 @@
     block[BODY:BLOCK, :] = meta.astype(jnp.float32).astype(jnp.bfloat16)
 
 
-def half_scores(rows, half, col_ref):
+def half_scores(rows, half, folded, col_ref):
     first = half * 8
     blocks = rows.shape[0] // BODY
     best = None
     tops = [[] for _ in range(blocks)]
-    for tile in range(8):
+    if folded:
+        pieces = [
+            [(chip, 2 * part + odd) for chip in (first + 2, first + 6) for odd in (1, 0)]
+            for part in range(8)
+        ]
+    else:
+        pieces = [[(first, part)] for part in range(16)]
+    width = 2 if folded else 8
+    for tile in range(len(pieces) // 2):
         keys = [
-            col_ref[first : first + 8, (2 * tile + k) * 16 : (2 * tile + k + 1) * 16, :].reshape(
-                128, DIM
-            )
-            for k in range(2)
+            col_ref[slot : slot + width, 16 * t : 16 * t + 16, :].reshape(16 * width, DIM)
+            for slot, t in pieces[2 * tile] + pieces[2 * tile + 1]
         ]
         scores = lax.dot_general(
             rows,
@@ -216,7 +222,7 @@
     for k in (3, 4, 1, 2):
         col_copies[k].start()
     core_copies[0].start()
-    row_waves = ((1, 2, 3), (4, 5, 6), (7, 8, 9))
+    row_waves = (tuple(range(1, 10)),)
     for k, wave in enumerate(row_waves):
         for r in row_waves[k - 1] if k else ():
             row_copies[r - 1].wait_send()
@@ -257,22 +263,28 @@
         row_side[r, 0] = jnp.broadcast_to(chosen[0:8], small)
         row_side[r, 1] = jnp.broadcast_to(chosen[8:16], small)
 
-    def pair_unit(p, half):
+    def pair_unit(p, half, folded=False):
         rows = row_ref[pl.ds(2 * p, 2), 0:BODY, :].reshape(2 * BODY, DIM)
-        bests, all_tops = half_scores(rows, half, col_ref)
+        bests, all_tops = half_scores(rows, half, folded, col_ref)
         found = []
         for q in range(2):
             r = 2 * p + q
             row_count, row_cluster = row_side[r, 0], row_side[r, 1]
-            best = roll_max(bests[q], (DIM - 4, DIM - 8), 1)
+            best = roll_max(bests[q], ((32,) if folded else ()) + (DIM - 4, DIM - 8), 1)
             forward = roll_sum(jnp.sum(best.reshape(BODY // 8, 8, DIM), axis=0), (4,), 0)
             start = jnp.where(sub < 4, best[0:8], pltpu.roll(best[0:8], 4, 0))
             forward = forward - (TOKS - row_count) * start
             tops = [roll_max(top, (4,), 0) for top in all_tops[q]]
-            backward = roll_sum(functools.reduce(jnp.add, tops), (DIM - 4, DIM - 8), 1)
+            backward = roll_sum(
+                functools.reduce(jnp.add, tops),
+                ((32,) if folded else ()) + (DIM - 4, DIM - 8),
+                1,
+            )
             backward = backward - (TOKS - key_count[half]) * tops[0]
             chamfer = factor * (forward / row_count + backward / key_count[half])
             distinct = lane % 16 < DOCS
+            if folded:
+                distinct = distinct & (lane // 32 % 2 == 1)
             if half == 0:
                 distinct = distinct & ~((lane // 16 == 0) & same_doc & (r == 0))
             partner = distinct & (key_cluster[half] == row_cluster)
@@ -282,39 +294,34 @@
             col_best[half, side] = jnp.maximum(col_best[half, side], top)
         return found
 
-    def row_copy(r):
-        return remote(row_ref.at[0], row_ref.at[r], row_send.at[r], row_recv.at[r], row_owner(r))
-
     def row_result(r):
         return remote(
             row_out.at[r], row_in.at[r], row_out_send.at[r], row_in_recv.at[r], row_owner(r)
         )
 
-    def first_half(p, state):
-        @pl.when(p > 0)
-        def _():
-            row_copy(2 * p).wait_recv()
-
-        row_copy(2 * p + 1).wait_recv()
-        for q in range(2):
-            row_meta(2 * p + q)
-        for q, found in enumerate(pair_unit(p, 0)):
-            row_best[2 * p + q, 0] = found[0]
-            row_best[2 * p + q, 1] = found[1]
-        return state
+    def first_half(pairs):
+        members = [2 * p + q for p in pairs for q in range(2)]
+        for r in members:
+            if r:
+                row_copies[r - 1].wait_recv()
+        for r in members:
+            row_meta(r)
+        for p in pairs:
+            for q, found in enumerate(pair_unit(p, 0)):
+                row_best[2 * p + q, 0] = found[0]
+                row_best[2 * p + q, 1] = found[1]
 
     def by_lane(value):
         top = jnp.broadcast_to(jnp.max(value, axis=1, keepdims=True), small)
         return roll_max(jnp.where(same_doc, top, NEG_FILL), (1, 2), 0)
 
-    def second_half(p, state):
-        for q, (overall, within) in enumerate(pair_unit(p, 1)):
+    def second_half(p):
+        for q, (overall, within) in enumerate(pair_unit(p, 1, p in FOLDED)):
             r = 2 * p + q
             overall = by_lane(jnp.maximum(overall, row_best[r, 0]))
             within = by_lane(jnp.maximum(within, row_best[r, 1]))
             row_out[r] = jnp.where(sub < 4, overall, within)
 
-        return state
 
     col_outs = [
         remote(
@@ -335,17 +342,19 @@
             col_outs[slot].start()
 
     read_meta(0)
-    lax.fori_loop(0, EARLY, first_half, 0)
+    first_half((0, 1))
+    first_half((2, 3))
     for k in (5, 6):
         col_copies[k].wait_recv()
         core_copies[k].start()
     col_copies[7].wait_recv()
     col_copies[0].wait_recv()
     core_copies[7].start()
-    lax.fori_loop(EARLY, N_ROWS // 2, first_half, 0)
+    first_half((4,))
     return_cols(0)
     read_meta(1)
-    lax.fori_loop(0, N_ROWS // 2, second_half, 0, unroll=True)
+    for p in range(N_ROWS // 2):
+        second_half(p)
     return_cols(1)
     for r in reversed(range(1, N_ROWS)):
         row_result(r).start()

time: 35.1 us -> 34.4 us (0.980)
  Pallas kernels: 32.9 us -> 32.3 us
    pallas_call x1, Pallas kernels: 32.9 us -> 32.3 us  [shards(): pl.pallas_call(kernel, out_shape=jax.ShapeDtypeStruct((8, DIM), jnp.float...]
where the time goes in v4:
time: 34.4 us; the launch traced here: 34.2 us
  Pallas kernels  32.3 us (94%)
  local copies, waits for them, and re-layouts  1.26 us (4%)
  between operations  0.64 us (2%)
    pallas_call x1, Pallas kernels, shards(): pl.pallas_call(kernel, out_shape=jax.ShapeDtypeStruct((8, DIM), jnp.float...  32.3 us
    squeeze x1, local copies, waits for them, and re-layouts, shards(): return (scores[0, :DOCS], scores[4, :DOCS])  1.26 us

profile of v4, /device:TPU:1, one launch (start us, length us, event | category | flops | bytes accessed | tf_op | source)
XLA Modules:
  0.0 34.2 jit_solution(7974409840055077642)
XLA Ops:
  0.6 32.3 %shard_map.59 = f32[8,128]{1,0:T(8,128)} custom-call(bf16[4,64,128]{2,1,0:T(8,128)(2,1)} %quantized_hbm.1, bf16[4,4,64]{2,1,0:T(4,128)(2,1)} %bitcast.5, s32[4]{0:T(128)} %counts_hbm.1, s32[4]{0:T(128)} %clusters_hbm.1), custom_call_target="tpu_custom_call" | custom-call | tf_op jit(solution)/shard_map/pallas_call | solution.py:383
  33.0 1.3 %slice_bitcast_fusion = (f32[4]{0:T(128)}, f32[4]{0:T(128)}) fusion(f32[8,128]{1,0:T(8,128)} %shard_map.59), kind=kLoop, calls=%fused_computation | loop fusion | bytes 64 | tf_op jit(solution)/shard_map/squeeze | solution.py:421

commit v5 on v4

--- a/solution.py
+++ b/solution.py
@@ -355,8 +355,11 @@
     read_meta(1)
     for p in range(N_ROWS // 2):
         second_half(p)
+        if p == 2:
+            for r in reversed(range(1, 6)):
+                row_result(r).start()
     return_cols(1)
-    for r in reversed(range(1, N_ROWS)):
+    for r in reversed(range(6, N_ROWS)):
         row_result(r).start()
 
     for copy in col_copies + [row_copies[r - 1] for r in row_waves[-1]] + core_copies:

time: 34.4 us -> 34.8 us (1.012)
  Pallas kernels: 32.3 us -> 32.8 us
    pallas_call x1, Pallas kernels: 32.3 us -> 32.8 us  [shards(): pl.pallas_call(kernel, out_shape=jax.ShapeDtypeStruct((8, DIM), jnp.float...]
where the time goes in v5:
time: 34.8 us; the launch traced here: 34.7 us
  Pallas kernels  32.8 us (94%)
  local copies, waits for them, and re-layouts  1.26 us (4%)
  between operations  0.64 us (2%)
    pallas_call x1, Pallas kernels, shards(): pl.pallas_call(kernel, out_shape=jax.ShapeDtypeStruct((8, DIM), jnp.float...  32.8 us
    squeeze x1, local copies, waits for them, and re-layouts, shards(): return (scores[0, :DOCS], scores[4, :DOCS])  1.26 us

profile of v5, /device:TPU:1, one launch (start us, length us, event | category | flops | bytes accessed | tf_op | source)
XLA Modules:
  0.0 34.7 jit_solution(694200073721936042)
XLA Ops:
  0.6 32.8 %shard_map.59 = f32[8,128]{1,0:T(8,128)} custom-call(bf16[4,64,128]{2,1,0:T(8,128)(2,1)} %quantized_hbm.1, bf16[4,4,64]{2,1,0:T(4,128)(2,1)} %bitcast.5, s32[4]{0:T(128)} %counts_hbm.1, s32[4]{0:T(128)} %clusters_hbm.1), custom_call_target="tpu_custom_call" | custom-call | tf_op jit(solution)/shard_map/pallas_call | solution.py:386
  33.4 1.3 %slice_bitcast_fusion = (f32[4]{0:T(128)}, f32[4]{0:T(128)}) fusion(f32[8,128]{1,0:T(8,128)} %shard_map.59), kind=kLoop, calls=%fused_computation | loop fusion | bytes 64 | tf_op jit(solution)/shard_map/squeeze | solution.py:424
